TPU v7x, 256 devices: a whole 4x4x8 slice. The times are simulated.
256 devices in a mesh: gx: 4 (over x_lo, core), gy: 8 (over y, x_hi), gz: 8 (over z).
Axes of the slice: x: 4 (x_hi: 2, x_lo: 2; x = x_hi * 2 + x_lo), y: 4, z: 8, core: 2. Of those that a mesh axis runs over, the one named last changes fastest.
Arguments:
- atoms: float32 [4, 4, 8, 512, 128], P(None, 'gx', 'gy', 'gz'), as said below
- velocities: float32 [3, 4, 8, 512, 128], P(None, 'gx', 'gy', 'gz'), may hold values from -4 to 4
- inverse_mass: float32 [4, 8, 512, 128], P('gx', 'gy', 'gz'), as said below
- bond_partner: int32 [4, 8, 512, 128], P('gx', 'gy', 'gz'), may hold values from 0 to 127, as said below
- cluster_pairs: int32 [2, 4, 8, 2048], P(None, 'gx', 'gy', 'gz'), may hold values from 0 to 575, as said below
- pair_count: int32 [4, 8, 8], P('gx', 'gy', 'gz'), may hold values from 64 to 256, as said below
Outputs:
- forces: float32 [3, 4, 8, 512, 128], P(None, 'gx', 'gy', 'gz')
- new_velocities: float32 [3, 4, 8, 512, 128], P(None, 'gx', 'gy', 'gz')
Inputs may be any that keep to these rules, and one draw needn't show every extreme that they name: `cluster_pairs`: row 0 names a tower slot below 192, row 1 a plate slot, in the slot numbering of the steps. Only the first pair_count slots of a device are live; the others hold arbitrary valid slots. No pair names the device's own cluster c twice (tower slot 64 + c with plate slot 256 + c). `pair_count`: some device has exactly 256 live pairs and some device exactly 64. `bond_partner`: A hydrogen names the heavy atom of its update group; every other atom names itself; no atom names a hydrogen. Update groups lie within aligned runs of four atoms of a cluster, whose first atom is heavy. `atoms`: A hydrogen lies 0.08 to 0.18 nm from the heavy atom it names. `inverse_mass`: 1 / 1.008 for hydrogens, 1 / 32 to 1 / 12 for other atoms.
All inputs are finite; a program needn't handle non-finite values.
Results may differ from a plain program's by a relative error of at most 0.0003.
Values sent between devices are 32-bit elements; how exact they have to be, the bound alone decides.
No kernel may reach another device: no remote copies, remote signals or barrier semaphores. Data moves between devices by JAX's collectives and lax.ppermute only.
A program may use at most 64 MiB of HBM per device.

v0:
```python
import jax
import jax.numpy as jnp
from jax import lax
from jax.sharding import PartitionSpec as P

ITERS = 2


TIME_STEP = 0.002
FORCE_UNIT = 500.0
CUTOFF = 1.2
SOFT_CORE = 0.04
EXACT = lax.Precision.HIGHEST


def passed_along(value, axis, steps):
    count = lax.axis_size(axis)
    pairs = [(source, (source + steps) % count) for source in range(count)]
    return lax.ppermute(value, axis, pairs)


def padded(cells, sides, width):
    for axis, dim in sides:
        count = lax.axis_size(axis)
        head = lax.slice_in_dim(cells, 0, width, axis=dim)
        tail = lax.slice_in_dim(cells, cells.shape[dim] - width, cells.shape[dim], axis=dim)
        cells = jnp.concatenate(
            [
                lax.ppermute(tail, axis, [(i, (i + 1) % count) for i in range(count)]),
                cells,
                lax.ppermute(head, axis, [((i + 1) % count, i) for i in range(count)]),
            ],
            axis=dim,
        )
    return cells


def edge_of(clusters):
    return 2.4 * (clusters / 8.0) ** (1.0 / 3.0)


def pair_kernel(tower_part, plate_part):
    apart = tower_part[:3, :, :, None] - plate_part[:3, :, None, :]
    spread = apart[0] * apart[0] + apart[1] * apart[1] + apart[2] * apart[2]
    weight = 1.0 / (spread + SOFT_CORE)
    taper = jnp.maximum(1.0 - spread * (1.0 / CUTOFF**2), 0.0)
    taper = taper * taper
    charges = tower_part[3, :, :, None] * plate_part[3, :, None, :]
    scalar = taper * charges * (weight * jnp.sqrt(weight) - 1.0 / CUTOFF**3)
    pulls = scalar[None] * apart
    return (jnp.sum(pulls, axis=3), -jnp.sum(pulls, axis=2))


def selector(rows, total):
    return (rows[:, None] == jnp.arange(total, dtype=jnp.int32)[None, :]).astype(jnp.float32)


def pick_rows(table, choose):
    return jnp.einsum("ns,ksw->knw", choose, table, precision=EXACT)


def spread_rows(values, choose):
    return jnp.einsum("ns,knw->ksw", choose, values, precision=EXACT)


def sweep_pairs(tower, plate, tower_index, plate_index, count, blocks):
    per_block = 32
    width = tower.shape[2]
    tower_slots = tower.shape[1]
    plate_slots = plate.shape[1]

    def visit(number, totals):
        tower_total, plate_total = totals
        first = number * per_block
        tower_rows = lax.dynamic_slice_in_dim(tower_index, first, per_block)
        plate_rows = lax.dynamic_slice_in_dim(plate_index, first, per_block)
        active = (first + jnp.arange(per_block, dtype=jnp.int32) < count).astype(jnp.float32)[
            :, None
        ]
        tower_pick = selector(tower_rows, tower_slots)
        plate_pick = selector(plate_rows, plate_slots)
        tower_pull, plate_pull = pair_kernel(
            pick_rows(tower, tower_pick), pick_rows(plate, plate_pick)
        )
        return (
            tower_total + spread_rows(tower_pull, tower_pick * active),
            plate_total + spread_rows(plate_pull, plate_pick * active),
        )

    start = (
        jnp.zeros((3, tower_slots, width), jnp.float32),
        jnp.zeros((3, plate_slots, width), jnp.float32),
    )
    return lax.fori_loop(0, blocks, visit, start)


def tower_back(piece, offset):
    return passed_along(piece, "gz", offset)


def along_rows(piece, offset):
    return passed_along(piece, "gy", offset)


def along_columns(piece, offset):
    return passed_along(piece, "gx", offset)


def hold_bonds(coords, kicked, inverse_mass, partner):
    place = jnp.arange(partner.shape[-1], dtype=jnp.int32)
    hydro = partner != place
    onehot = (partner[:, :, None] == place).astype(jnp.float32)

    def partner_of(values):
        return jnp.einsum("kcp,chp->kch", values, onehot, precision=EXACT)

    bond = coords - partner_of(coords)
    bond_square = jnp.sum(bond * bond, axis=0)
    paired = inverse_mass + partner_of(inverse_mass[None])[0]
    shift = TIME_STEP * kicked
    for sweep in range(ITERS):
        gap = bond + (shift - partner_of(shift))
        excess = jnp.sum(gap * gap, axis=0) - bond_square
        slope = 2.0 * jnp.sum(gap * bond, axis=0) * paired
        factor = jnp.where(hydro, excess / jnp.where(hydro, slope, 1.0), 0.0)
        delta = factor[None] * bond
        back = jnp.einsum("kch,chp->kcp", delta, onehot, precision=EXACT)
        shift = shift + inverse_mass[None] * (back - delta)
    return shift / TIME_STEP


def local(atoms, velocities, inverse_mass, bond_partner, cluster_pairs, pair_count):
    clusters = atoms.shape[3]
    width = atoms.shape[4]
    edge = edge_of(clusters)
    tower = padded(atoms, (("gz", 3),), clusters)
    tower = tower.reshape(4, 3 * clusters, width)
    zones = jnp.arange(3 * clusters, dtype=jnp.int32) // clusters
    lift = (zones - 1).astype(jnp.float32) * edge
    nothing = jnp.zeros_like(lift)
    tower = tower + jnp.stack([nothing, nothing, lift, nothing])[:, :, None]
    plate = padded(atoms, (("gx", 1), ("gy", 2)), 1)
    plate = plate.reshape(4, 9 * clusters, width)
    cells = jnp.arange(9 * clusters, dtype=jnp.int32) // clusters
    lift_across = (cells // 3 - 1).astype(jnp.float32) * edge
    lift_along = (cells % 3 - 1).astype(jnp.float32) * edge
    blank = jnp.zeros_like(lift_across)
    plate = plate + jnp.stack([lift_across, lift_along, blank, blank])[:, :, None]
    tower_index = cluster_pairs[0, 0, 0]
    plate_index = cluster_pairs[1, 0, 0]
    count = pair_count[0, 0, 0]
    tower_force, plate_force = sweep_pairs(
        tower, plate, tower_index, plate_index, count, (count + 31) // 32
    )
    forces = (
        tower_force[:, clusters : 2 * clusters]
        + tower_back(tower_force[:, :clusters], -1)
        + tower_back(tower_force[:, 2 * clusters :], 1)
    )
    grid = plate_force.reshape(3, 3, 3, clusters, width)
    lines = grid[:, :, 1] + along_rows(grid[:, :, 0], -1) + along_rows(grid[:, :, 2], 1)
    plate_own = lines[:, 1] + along_columns(lines[:, 0], -1) + along_columns(lines[:, 2], 1)
    forces = forces + plate_own
    coords = atoms[:3, 0, 0]
    kicked = velocities[:, 0, 0] + TIME_STEP * FORCE_UNIT * inverse_mass[0, 0][None] * forces
    moved = hold_bonds(coords, kicked, inverse_mass[0, 0], bond_partner[0, 0])
    return (forces[:, None, None], moved[:, None, None])


def solution(mesh):
    return jax.shard_map(
        local,
        mesh=mesh,
        in_specs=(
            P(None, "gx", "gy", "gz", None),
            P(None, "gx", "gy", "gz", None),
            P("gx", "gy", "gz", None),
            P("gx", "gy", "gz", None),
            P(None, "gx", "gy", "gz"),
            P("gx", "gy", "gz"),
        ),
        out_specs=(P(None, "gx", "gy", "gz", None), P(None, "gx", "gy", "gz", None)),
        check_vma=False,
    )
```

profile of v0, /device:TPU:133, one launch (start us, length us, event | category | flops | bytes accessed | tf_op | source)
XLA Modules:
  0.0 159.4 jit_solution(1774664447639156030)
XLA Ops:
  2.9 1.9 %collective-permute-start.1 = (f32[4,1,1,64,128]{4,3,0,2,1:T(8,128)}, f32[4,1,1,64,128]{4,3,0,2,1:T(8,128)S(1)}, u32[]{:S(2)}, u32[]{:S(2)}) collective-permute-start(f32[4,1,1,64,128]{4,3,0,2,1:T(8,128)} %bitcast.174), channel_id=1, source_target_pairs={{1,0},{2,1},{3,2},{4,3},{5,4},{6,5},{7,6},{0,7},{9,8},{10,9},{11,1... | collective-permute-start | bytes 393224 | tf_op jit(solution)/shard_map/ppermute | solution.py:31
  12.6 5.9 %collective-permute-done.4 = f32[4,3,1,64,128]{4,3,2,1,0:T(8,128)S(1)} collective-permute-done((f32[4,3,1,64,128]{4,3,2,1,0:T(8,128)S(1)}, f32[4,3,1,64,128]{4,3,2,1,0:T(8,128)S(1)}, u32[]{:S(2)}, u32[]{:S(2)}) %collective-permute-start.4) | collective-permute-done | bytes 393248 | tf_op jit(solution)/shard_map/ppermute | solution.py:29
  18.4 9.4 %collective-permute-done.5 = f32[4,3,1,64,128]{4,3,2,1,0:T(8,128)S(1)} collective-permute-done((f32[4,3,1,64,128]{4,3,2,1,0:T(8,128)S(1)}, f32[4,3,1,64,128]{4,3,2,1,0:T(8,128)S(1)}, u32[]{:S(2)}, u32[]{:S(2)}) %collective-permute-start.5) | collective-permute-done | bytes 393248 | tf_op jit(solution)/shard_map/ppermute | solution.py:31
  28.4 87.9 %while.14 = (s32[]{:T(128)}, f32[3,192,128]{2,1,0:T(8,128)S(1)}, f32[3,576,128]{2,1,0:T(8,128)S(1)}, s32[]{:T(128)}, s32[256]{0:T(256)S(1)}, /*index=5*/f32[4,19...) while((s32[]{:T(128)}, f32[3,192,128]{2,1,0:T(8,128)S(1)}, ...), condition=%wide.region_3.4_spmd, body=%wide.region_0.3_spmd.sunk | while | flops 280850528 | bytes 21530172 | solution.py:94
  29.5 1.8 %broadcast_subtract_fusion.2 = f32[3,32,128,128]{3,2,1,0:T(8,128)S(1)} fusion(f32[3,32,128]{2,1,0:T(8,128)S(1)} %slice.159, f32[3,32,128]{2,1,0:T(8,128)S(1)} %slice.160), kind=kLoop, calls=%fused_computation.3.clone.1 | loop fusion | flops 1572864 | bytes 6389760 | tf_op jit(solution)/shard_map/while/body/sub | solution.py:43
  32.9 4.0 %multiply_reduce_fusion.8 = (f32[3,32,128]{2,1,0:T(8,128)S(1)}, f32[3,32,128]{2,1,0:T(8,128)S(1)}) fusion(f32[32,128,128]{2,1,0:T(8,128)S(1)} %fusion.104, f32[3,32,128]{2,1,0:T(8,128)S(1)} %slice.159, f32[3,32,128]{2,1,0:T(8,128)S(1)} %slice.160), kind=kLoop, calls=%fused_computation.clone.1 | loop fusion | flops 6266880 | bytes 2293760 | tf_op jit(solution)/shard_map/while/body/reduce_sum | solution.py:51
  40.5 1.8 %broadcast_subtract_fusion.2 = f32[3,32,128,128]{3,2,1,0:T(8,128)S(1)} fusion(f32[3,32,128]{2,1,0:T(8,128)S(1)} %slice.159, f32[3,32,128]{2,1,0:T(8,128)S(1)} %slice.160), kind=kLoop, calls=%fused_computation.3.clone.1 | loop fusion | flops 1572864 | bytes 6389760 | tf_op jit(solution)/shard_map/while/body/sub | solution.py:43
  42.3 1.6 %fusion.104 = f32[32,128,128]{2,1,0:T(8,128)S(1)} fusion(f32[3,32,128,128]{3,2,1,0:T(8,128)S(1)} %broadcast_subtract_fusion.2, f32[32,128]{1,0:T(8,128)S(1)} %get-tuple-element.229, f32[32,128]{1,0:T(8,128)S(1)} %get-tuple-element.230), kind=kLoop, calls=%fused_computation.6.clone.1 | loop fusion | flops 8388608 | bytes 8421376 | tf_op jit(solution)/shard_map/while/body/mul | solution.py:50
  43.9 4.0 %multiply_reduce_fusion.8 = (f32[3,32,128]{2,1,0:T(8,128)S(1)}, f32[3,32,128]{2,1,0:T(8,128)S(1)}) fusion(f32[32,128,128]{2,1,0:T(8,128)S(1)} %fusion.104, f32[3,32,128]{2,1,0:T(8,128)S(1)} %slice.159, f32[3,32,128]{2,1,0:T(8,128)S(1)} %slice.160), kind=kLoop, calls=%fused_computation.clone.1 | loop fusion | flops 6266880 | bytes 2293760 | tf_op jit(solution)/shard_map/while/body/reduce_sum | solution.py:51
  51.4 1.8 %broadcast_subtract_fusion.2 = f32[3,32,128,128]{3,2,1,0:T(8,128)S(1)} fusion(f32[3,32,128]{2,1,0:T(8,128)S(1)} %slice.159, f32[3,32,128]{2,1,0:T(8,128)S(1)} %slice.160), kind=kLoop, calls=%fused_computation.3.clone.1 | loop fusion | flops 1572864 | bytes 6389760 | tf_op jit(solution)/shard_map/while/body/sub | solution.py:43
  53.2 1.6 %fusion.104 = f32[32,128,128]{2,1,0:T(8,128)S(1)} fusion(f32[3,32,128,128]{3,2,1,0:T(8,128)S(1)} %broadcast_subtract_fusion.2, f32[32,128]{1,0:T(8,128)S(1)} %get-tuple-element.229, f32[32,128]{1,0:T(8,128)S(1)} %get-tuple-element.230), kind=kLoop, calls=%fused_computation.6.clone.1 | loop fusion | flops 8388608 | bytes 8421376 | tf_op jit(solution)/shard_map/while/body/mul | solution.py:50
  54.9 4.0 %multiply_reduce_fusion.8 = (f32[3,32,128]{2,1,0:T(8,128)S(1)}, f32[3,32,128]{2,1,0:T(8,128)S(1)}) fusion(f32[32,128,128]{2,1,0:T(8,128)S(1)} %fusion.104, f32[3,32,128]{2,1,0:T(8,128)S(1)} %slice.159, f32[3,32,128]{2,1,0:T(8,128)S(1)} %slice.160), kind=kLoop, calls=%fused_computation.clone.1 | loop fusion | flops 6266880 | bytes 2293760 | tf_op jit(solution)/shard_map/while/body/reduce_sum | solution.py:51
  62.4 1.8 %broadcast_subtract_fusion.2 = f32[3,32,128,128]{3,2,1,0:T(8,128)S(1)} fusion(f32[3,32,128]{2,1,0:T(8,128)S(1)} %slice.159, f32[3,32,128]{2,1,0:T(8,128)S(1)} %slice.160), kind=kLoop, calls=%fused_computation.3.clone.1 | loop fusion | flops 1572864 | bytes 6389760 | tf_op jit(solution)/shard_map/while/body/sub | solution.py:43
  65.9 4.0 %multiply_reduce_fusion.8 = (f32[3,32,128]{2,1,0:T(8,128)S(1)}, f32[3,32,128]{2,1,0:T(8,128)S(1)}) fusion(f32[32,128,128]{2,1,0:T(8,128)S(1)} %fusion.104, f32[3,32,128]{2,1,0:T(8,128)S(1)} %slice.159, f32[3,32,128]{2,1,0:T(8,128)S(1)} %slice.160), kind=kLoop, calls=%fused_computation.clone.1 | loop fusion | flops 6266880 | bytes 2293760 | tf_op jit(solution)/shard_map/while/body/reduce_sum | solution.py:51
  73.4 1.8 %broadcast_subtract_fusion.2 = f32[3,32,128,128]{3,2,1,0:T(8,128)S(1)} fusion(f32[3,32,128]{2,1,0:T(8,128)S(1)} %slice.159, f32[3,32,128]{2,1,0:T(8,128)S(1)} %slice.160), kind=kLoop, calls=%fused_computation.3.clone.1 | loop fusion | flops 1572864 | bytes 6389760 | tf_op jit(solution)/shard_map/while/body/sub | solution.py:43
  75.2 1.6 %fusion.104 = f32[32,128,128]{2,1,0:T(8,128)S(1)} fusion(f32[3,32,128,128]{3,2,1,0:T(8,128)S(1)} %broadcast_subtract_fusion.2, f32[32,128]{1,0:T(8,128)S(1)} %get-tuple-element.229, f32[32,128]{1,0:T(8,128)S(1)} %get-tuple-element.230), kind=kLoop, calls=%fused_computation.6.clone.1 | loop fusion | flops 8388608 | bytes 8421376 | tf_op jit(solution)/shard_map/while/body/mul | solution.py:50
  76.9 4.0 %multiply_reduce_fusion.8 = (f32[3,32,128]{2,1,0:T(8,128)S(1)}, f32[3,32,128]{2,1,0:T(8,128)S(1)}) fusion(f32[32,128,128]{2,1,0:T(8,128)S(1)} %fusion.104, f32[3,32,128]{2,1,0:T(8,128)S(1)} %slice.159, f32[3,32,128]{2,1,0:T(8,128)S(1)} %slice.160), kind=kLoop, calls=%fused_computation.clone.1 | loop fusion | flops 6266880 | bytes 2293760 | tf_op jit(solution)/shard_map/while/body/reduce_sum | solution.py:51
  84.4 1.8 %broadcast_subtract_fusion.2 = f32[3,32,128,128]{3,2,1,0:T(8,128)S(1)} fusion(f32[3,32,128]{2,1,0:T(8,128)S(1)} %slice.159, f32[3,32,128]{2,1,0:T(8,128)S(1)} %slice.160), kind=kLoop, calls=%fused_computation.3.clone.1 | loop fusion | flops 1572864 | bytes 6389760 | tf_op jit(solution)/shard_map/while/body/sub | solution.py:43
  87.8 4.0 %multiply_reduce_fusion.8 = (f32[3,32,128]{2,1,0:T(8,128)S(1)}, f32[3,32,128]{2,1,0:T(8,128)S(1)}) fusion(f32[32,128,128]{2,1,0:T(8,128)S(1)} %fusion.104, f32[3,32,128]{2,1,0:T(8,128)S(1)} %slice.159, f32[3,32,128]{2,1,0:T(8,128)S(1)} %slice.160), kind=kLoop, calls=%fused_computation.clone.1 | loop fusion | flops 6266880 | bytes 2293760 | tf_op jit(solution)/shard_map/while/body/reduce_sum | solution.py:51
  95.4 1.8 %broadcast_subtract_fusion.2 = f32[3,32,128,128]{3,2,1,0:T(8,128)S(1)} fusion(f32[3,32,128]{2,1,0:T(8,128)S(1)} %slice.159, f32[3,32,128]{2,1,0:T(8,128)S(1)} %slice.160), kind=kLoop, calls=%fused_computation.3.clone.1 | loop fusion | flops 1572864 | bytes 6389760 | tf_op jit(solution)/shard_map/while/body/sub | solution.py:43
  98.8 4.0 %multiply_reduce_fusion.8 = (f32[3,32,128]{2,1,0:T(8,128)S(1)}, f32[3,32,128]{2,1,0:T(8,128)S(1)}) fusion(f32[32,128,128]{2,1,0:T(8,128)S(1)} %fusion.104, f32[3,32,128]{2,1,0:T(8,128)S(1)} %slice.159, f32[3,32,128]{2,1,0:T(8,128)S(1)} %slice.160), kind=kLoop, calls=%fused_computation.clone.1 | loop fusion | flops 6266880 | bytes 2293760 | tf_op jit(solution)/shard_map/while/body/reduce_sum | solution.py:51
  106.3 1.8 %broadcast_subtract_fusion.2 = f32[3,32,128,128]{3,2,1,0:T(8,128)S(1)} fusion(f32[3,32,128]{2,1,0:T(8,128)S(1)} %slice.159, f32[3,32,128]{2,1,0:T(8,128)S(1)} %slice.160), kind=kLoop, calls=%fused_computation.3.clone.1 | loop fusion | flops 1572864 | bytes 6389760 | tf_op jit(solution)/shard_map/while/body/sub | solution.py:43
  109.8 4.0 %multiply_reduce_fusion.8 = (f32[3,32,128]{2,1,0:T(8,128)S(1)}, f32[3,32,128]{2,1,0:T(8,128)S(1)}) fusion(f32[32,128,128]{2,1,0:T(8,128)S(1)} %fusion.104, f32[3,32,128]{2,1,0:T(8,128)S(1)} %slice.159, f32[3,32,128]{2,1,0:T(8,128)S(1)} %slice.160), kind=kLoop, calls=%fused_computation.clone.1 | loop fusion | flops 6266880 | bytes 2293760 | tf_op jit(solution)/shard_map/while/body/reduce_sum | solution.py:51
  117.7 3.3 %collective-permute-start.9 = (f32[3,3,64,128]{3,0,2,1:T(4,128)S(1)}, f32[3,3,64,128]{3,0,2,1:T(4,128)S(1)}, u32[]{:S(2)}, u32[]{:S(2)}) collective-permute-start(f32[3,3,64,128]{3,0,2,1:T(4,128)S(1)} %bitcast.178), channel_id=1, source_target_pairs={{0,8},{8,16},{16,24},{24,32},{32,40},{40,48},{48,56},{56,0},{1,9},... | collective-permute-start | bytes 884744 | tf_op jit(solution)/shard_map/ppermute | solution.py:19
  121.0 4.0 %fusion.39 = f32[3,64,128]{2,0,1:T(4,128)S(1)} fusion(s32[64,128]{1,0:T(8,128)S(1)} %bitcast.185, f32[3,1,1,64,128]{4,3,2,1,0:T(8,128)S(1)} %slice.92), kind=kOutput, calls=%fused_computation.56 | convolution fusion | flops 38821888 | bytes 229376 | tf_op jit(solution)/shard_map/kcp,chp->kch/dot_general | solution.py:115
  127.3 10.3 %collective-permute-done.9 = f32[3,3,64,128]{3,0,2,1:T(4,128)S(1)} collective-permute-done((f32[3,3,64,128]{3,0,2,1:T(4,128)S(1)}, f32[3,3,64,128]{3,0,2,1:T(4,128)S(1)}, u32[]{:S(2)}, u32[]{:S(2)}) %collective-permute-start.9) | collective-permute-done | bytes 294944 | tf_op jit(solution)/shard_map/ppermute | solution.py:19
  138.0 1.8 %collective-permute-start.11 = (f32[3,64,128]{2,0,1:T(4,128)S(1)}, f32[3,64,128]{2,0,1:T(4,128)S(1)}, u32[]{:S(2)}, u32[]{:S(2)}) collective-permute-start(f32[3,64,128]{2,0,1:T(4,128)S(1)} %get-tuple-element.162), channel_id=1, source_target_pairs={{0,64},{64,128},{128,192},{192,0},{1,65},{65,129},{129,193},{193,1... | collective-permute-start | bytes 294920 | tf_op jit(solution)/shard_map/ppermute | solution.py:19
  139.8 4.0 %fusion.29 = f32[64,1,128]{2,1,0:T(1,128)S(1)} fusion(f32[64,128,1]{1,2,0:T(1,128)S(1)} %bitcast.179, s32[64,128]{1,0:T(8,128)S(1)} %bitcast.186), kind=kOutput, calls=%fused_computation.44 | convolution fusion | flops 13631488 | bytes 98304 | tf_op jit(solution)/shard_map/kcp,chp->kch/dot_general | solution.py:115
  143.9 4.1 %multiply_reduce_fusion.5 = (f32[64,128]{1,0:T(8,128)S(1)}, f32[64,128]{1,0:T(8,128)S(1)}, f32[64,128]{1,0:T(8,128)S(1)}) fusion(f32[3,64,128]{2,0,1:T(4,128)S(1)} %fusion.39, f32[3,1,1,64,128]{4,3,2,1,0:T(8,128)S(1)} %copy-done.2, f32[3,64,128]{2,0,1:T(4,128)S(1)} %fusion.61, f32[64,128]{1,0:T(8,128)S(1)} %bitcast.180, s32[64,128]{1,0:T(8,128)S(1)} %bitcast.187), kind=kOutput, calls=%fused_computation.96 | convolution fusion | flops 39116800 | bytes 458752 | tf_op jit(solution)/shard_map/kcp,chp->kch/dot_general | solution.py:115
  148.0 2.9 %fusion.55 = f32[3,64,128]{2,0,1:T(4,128)S(1)} fusion(s32[64,128]{1,0:T(8,128)S(1)} %bitcast.188, f32[3,64,128]{2,0,1:T(4,128)S(1)} %fusion.39, f32[64,128]{1,0:T(8,128)S(1)} %get-tuple-element.152, f32[64,128]{1,0:T(8,128)S(1)} %bitcast.181, f32[3,64,128]{2,0,1:T(4,128)S(1)} %fusion.61, f32[3,1,1,64,128]{4,3,2,1,0:T(8,128)S(1)} %copy-done.2), kind=kOutput, calls=%fused_computation.72 | convolution fusion | flops 38993920 | bytes 491520 | tf_op jit(solution)/shard_map/kch,chp->kcp/dot_general | solution.py:127
  151.0 4.1 %multiply_reduce_fusion.3 = (f32[64,128]{1,0:T(8,128)S(1)}, f32[64,128]{1,0:T(8,128)S(1)}) fusion(f32[3,64,128]{2,0,1:T(4,128)S(1)} %fusion.39, f32[3,64,128]{2,0,1:T(4,128)S(1)} %fusion.55, s32[64,128]{1,0:T(8,128)S(1)} %bitcast.189), kind=kOutput, calls=%fused_computation.93 | convolution fusion | flops 38928384 | bytes 294912 | tf_op jit(solution)/shard_map/kcp,chp->kch/dot_general | solution.py:115
  155.1 2.9 %fusion.54 = f32[3,1,1,64,128]{4,0,3,2,1:T(4,128)S(1)} fusion(f32[3,64,128]{2,0,1:T(4,128)S(1)} %fusion.55, s32[64,128]{1,0:T(8,128)S(1)} %bitcast.190, f32[3,64,128]{2,0,1:T(4,128)S(1)} %fusion.39, f32[64,128]{1,0:T(8,128)S(1)} %divide_select_fusion, f32[64,128]{1,0:T(8,128)S(1)} %bitcast.182), kind=kOutput, calls=%fused_computation.71 | convolution fusion | flops 38944768 | bytes 393216 | tf_op jit(solution)/shard_map/kch,chp->kcp/dot_general | solution.py:127
  (138 shorter events, 51.5 us)
Async XLA Ops:
  0.6 6.1 %collective-permute-start.2 = (f32[4,1,1,64,128]{4,3,2,1,0:T(8,128)}, f32[4,1,1,64,128]{4,3,2,1,0:T(8,128)S(1)}, u32[]{:S(2)}, u32[]{:S(2)}) collective-permute-start(f32[4,1,1,64,128]{4,3,2,1,0:T(8,128)} %param.8), channel_id=1, source_target_pairs={{0,64},{64,128},{128,192},{192,0},{1,65},{65,129},{129,193},{193,1... | collective-permute-start | bytes 393224 | tf_op jit(solution)/shard_map/ppermute | solution.py:29
  2.2 5.5 %collective-permute-start.3 = (f32[4,1,1,64,128]{4,3,2,1,0:T(8,128)}, f32[4,1,1,64,128]{4,3,2,1,0:T(8,128)S(1)}, u32[]{:S(2)}, u32[]{:S(2)}) collective-permute-start(f32[4,1,1,64,128]{4,3,2,1,0:T(8,128)} %param.8), channel_id=1, source_target_pairs={{64,0},{128,64},{192,128},{0,192},{65,1},{129,65},{193,129},{1,193... | collective-permute-start | bytes 393224 | tf_op jit(solution)/shard_map/ppermute | solution.py:31
  2.2 9.3 %collective-permute-start = (f32[4,1,1,64,128]{4,3,0,2,1:T(8,128)}, f32[4,1,1,64,128]{4,3,0,2,1:T(8,128)S(1)}, u32[]{:S(2)}, u32[]{:S(2)}) collective-permute-start(f32[4,1,1,64,128]{4,3,0,2,1:T(8,128)} %bitcast.173), channel_id=1, source_target_pairs={{0,1},{1,2},{2,3},{3,4},{4,5},{5,6},{6,7},{7,0},{8,9},{9,10},{10,1... | collective-permute-start | bytes 393224 | tf_op jit(solution)/shard_map/ppermute | solution.py:29
  2.9 8.6 %collective-permute-start.1 = (f32[4,1,1,64,128]{4,3,0,2,1:T(8,128)}, f32[4,1,1,64,128]{4,3,0,2,1:T(8,128)S(1)}, u32[]{:S(2)}, u32[]{:S(2)}) collective-permute-start(f32[4,1,1,64,128]{4,3,0,2,1:T(8,128)} %bitcast.174), channel_id=1, source_target_pairs={{1,0},{2,1},{3,2},{4,3},{5,4},{6,5},{7,6},{0,7},{9,8},{10,9},{11,1... | collective-permute-start | bytes 393224 | tf_op jit(solution)/shard_map/ppermute | solution.py:31
  7.7 10.7 %collective-permute-start.4 = (f32[4,3,1,64,128]{4,3,2,1,0:T(8,128)S(1)}, f32[4,3,1,64,128]{4,3,2,1,0:T(8,128)S(1)}, u32[]{:S(2)}, u32[]{:S(2)}) collective-permute-start(f32[4,3,1,64,128]{4,3,2,1,0:T(8,128)S(1)} %constant_dynamic-update-slice_fusion), channel_id=1, source_target_pairs={{0,8},{8,16},{16,24},{24,32},{32,40},{40,48},{48,56},{56,0},{1,9},... | collective-permute-start | bytes 1179656 | tf_op jit(solution)/shard_map/ppermute | solution.py:29
  9.4 18.5 %collective-permute-start.5 = (f32[4,3,1,64,128]{4,3,2,1,0:T(8,128)S(1)}, f32[4,3,1,64,128]{4,3,2,1,0:T(8,128)S(1)}, u32[]{:S(2)}, u32[]{:S(2)}) collective-permute-start(f32[4,3,1,64,128]{4,3,2,1,0:T(8,128)S(1)} %constant_dynamic-update-slice_fusion), channel_id=1, source_target_pairs={{8,0},{16,8},{24,16},{32,24},{40,32},{48,40},{56,48},{0,56},{9,1},... | collective-permute-start | bytes 1179656 | tf_op jit(solution)/shard_map/ppermute | solution.py:31
  116.3 4.7 %copy-start.1 = (s32[1,1,64,128]{3,2,1,0:T(8,128)S(1)}, s32[1,1,64,128]{3,2,1,0:T(8,128)}, u32[]{:S(2)}) copy-start(s32[1,1,64,128]{3,2,1,0:T(8,128)} %param.11) | copy-start | bytes 98308
  116.6 10.7 %collective-permute-start.8 = (f32[3,3,64,128]{3,0,2,1:T(4,128)S(1)}, f32[3,3,64,128]{3,0,2,1:T(4,128)S(1)}, u32[]{:S(2)}, u32[]{:S(2)}) collective-permute-start(f32[3,3,64,128]{3,0,2,1:T(4,128)S(1)} %bitcast.177), channel_id=1, source_target_pairs={{0,56},{8,0},{16,8},{24,16},{32,24},{40,32},{48,40},{56,48},{1,57}... | collective-permute-start | bytes 884744 | tf_op jit(solution)/shard_map/ppermute | solution.py:19
  117.7 19.9 %collective-permute-start.9 = (f32[3,3,64,128]{3,0,2,1:T(4,128)S(1)}, f32[3,3,64,128]{3,0,2,1:T(4,128)S(1)}, u32[]{:S(2)}, u32[]{:S(2)}) collective-permute-start(f32[3,3,64,128]{3,0,2,1:T(4,128)S(1)} %bitcast.178), channel_id=1, source_target_pairs={{0,8},{8,16},{16,24},{24,32},{32,40},{40,48},{48,56},{56,0},{1,9},... | collective-permute-start | bytes 884744 | tf_op jit(solution)/shard_map/ppermute | solution.py:19
  125.0 14.8 %copy-start = (f32[1,1,64,128]{3,2,1,0:T(8,128)S(1)}, f32[1,1,64,128]{3,2,1,0:T(8,128)}, u32[]{:S(2)}) copy-start(f32[1,1,64,128]{3,2,1,0:T(8,128)} %param.10) | copy-start | bytes 98308
  125.3 18.5 %collective-permute-start.6 = (f32[3,64,128]{2,0,1:T(4,128)S(1)}, f32[3,64,128]{2,0,1:T(4,128)S(1)}, u32[]{:S(2)}, u32[]{:S(2)}) collective-permute-start(f32[3,64,128]{2,0,1:T(4,128)S(1)} %get-tuple-element.159), channel_id=1, source_target_pairs={{0,7},{1,0},{2,1},{3,2},{4,3},{5,4},{6,5},{7,6},{8,15},{9,8},{10,9... | collective-permute-start | bytes 294920 | tf_op jit(solution)/shard_map/ppermute | solution.py:19
  125.4 18.4 %collective-permute-start.7 = (f32[3,64,128]{2,0,1:T(4,128)S(1)}, f32[3,64,128]{2,0,1:T(4,128)S(1)}, u32[]{:S(2)}, u32[]{:S(2)}) collective-permute-start(f32[3,64,128]{2,0,1:T(4,128)S(1)} %get-tuple-element.160), channel_id=1, source_target_pairs={{0,1},{1,2},{2,3},{3,4},{4,5},{5,6},{6,7},{7,0},{8,9},{9,10},{10,1... | collective-permute-start | bytes 294920 | tf_op jit(solution)/shard_map/ppermute | solution.py:19
  137.8 6.0 %copy-start.2 = (f32[3,1,1,64,128]{4,3,2,1,0:T(8,128)S(1)}, f32[3,1,1,64,128]{4,3,2,1,0:T(8,128)}, u32[]{:S(2)}) copy-start(f32[3,1,1,64,128]{4,3,2,1,0:T(8,128)} %param.9) | copy-start | bytes 294916
  137.9 5.9 %collective-permute-start.10 = (f32[3,64,128]{2,0,1:T(4,128)S(1)}, f32[3,64,128]{2,0,1:T(4,128)S(1)}, u32[]{:S(2)}, u32[]{:S(2)}) collective-permute-start(f32[3,64,128]{2,0,1:T(4,128)S(1)} %get-tuple-element.161), channel_id=1, source_target_pairs={{0,192},{64,0},{128,64},{192,128},{1,193},{65,1},{129,65},{193,129... | collective-permute-start | bytes 294920 | tf_op jit(solution)/shard_map/ppermute | solution.py:19
  138.0 5.8 %collective-permute-start.11 = (f32[3,64,128]{2,0,1:T(4,128)S(1)}, f32[3,64,128]{2,0,1:T(4,128)S(1)}, u32[]{:S(2)}, u32[]{:S(2)}) collective-permute-start(f32[3,64,128]{2,0,1:T(4,128)S(1)} %get-tuple-element.162), channel_id=1, source_target_pairs={{0,64},{64,128},{128,192},{192,0},{1,65},{65,129},{129,193},{193,1... | collective-permute-start | bytes 294920 | tf_op jit(solution)/shard_map/ppermute | solution.py:19
where the time goes:
time: 160 us; the launch traced here: 159 us
  other arithmetic  66.4 us (42%)
  matrix products  43.4 us (27%)
  waiting for transfers between devices  26 us (16%)
  starting transfers between devices  14.9 us (9%)
  local copies, waits for them, and re-layouts  6.24 us (4%)
    reduce_sum x8, other arithmetic, pair_kernel(): return (jnp.sum(pulls, axis=3), -jnp.sum(pulls, axis=2))  31.6 us
    dot_general x4, matrix products, partner_of(): return jnp.einsum('kcp,chp->kch', values, onehot, precision=EXACT)  16.2 us
    dot_general x16, matrix products, spread_rows(): return jnp.einsum('ns,knw->ksw', choose, values, precision=EXACT)  14.7 us
    sub x8, other arithmetic, pair_kernel(): apart = tower_part[:3, :, :, None] - plate_part[:3, :, None, :]  14.3 us
    mul x8, other arithmetic, pair_kernel(): pulls = scalar[None] * apart  13.1 us
    ppermute x6, waiting for transfers between devices, passed_along(): return lax.ppermute(value, axis, pairs)  10.7 us
    ppermute x3, waiting for transfers between devices, padded(): lax.ppermute(head, axis, [((i + 1) % count, i) for i in range(count)])  9.44 us
    ppermute x6, starting transfers between devices, passed_along(): return lax.ppermute(value, axis, pairs)  7.59 us
  transfers between devices with their start and end apart: 12, of which 4 were waited for; matrix products, arithmetic and copies ran while one was open for 8% of the time, Pallas kernels for 0%

commit v1 on v0

v1 whole, which is shorter than its diff:
```python
import functools

import jax
import jax.numpy as jnp
from jax import lax
from jax.experimental import pallas as pl
from jax.experimental.pallas import tpu as pltpu
from jax.sharding import PartitionSpec as P

ITERS = 2
TIME_STEP = 0.002
FORCE_UNIT = 500.0
CUTOFF = 1.2
SOFT_CORE = 0.04
SCALE = 1.0 / CUTOFF
CORE = SOFT_CORE / CUTOFF**2
STRENGTH = 1.0 / CUTOFF**2
HIGH, LOW = 8, 16
BLOCK = 2
SLOTS = 272
FIRST_OWN = 48
f32 = jnp.float32


def passed_along(value, axis, steps):
    count = lax.axis_size(axis)
    pairs = [(source, (source + steps) % count) for source in range(count)]
    return lax.ppermute(value, axis, pairs)


def plus(total, term):
    return term if total is None else total + term


def turned(value, shift):
    return value if shift % 128 == 0 else pltpu.roll(value, shift % 128, 1)


def eight_pairs(tower, plate, spun, pulled):
    tower_planes = [tower[8 * c : 8 * c + 8, :] for c in range(4)]
    plate_planes = [plate[8 * c : 8 * c + 8, :] for c in range(4)]
    tower_force = [None] * 3
    plate_force = [None] * 3
    rounds = HIGH // BLOCK
    for turn in range(rounds):
        coarse = [turn * BLOCK + u for u in range(BLOCK)]
        ahead = [[turned(v, -LOW * h) for v in tower_planes] for h in coarse]
        held = [[None] * 3 for _ in coarse]
        for low in range(LOW):
            if turn == 0:
                beside = [turned(v, low) for v in plate_planes]
                for c in range(4):
                    spun[low * 4 + c] = beside[c]
            else:
                beside = [spun[low * 4 + c] for c in range(4)]
            totals = [None if turn == 0 else pulled[low * 3 + c] for c in range(3)]
            for u in range(BLOCK):
                apart = [ahead[u][c] - beside[c] for c in range(3)]
                spread = apart[0] * apart[0] + apart[1] * apart[1] + apart[2] * apart[2]
                root = lax.rsqrt(spread + CORE)
                taper = jnp.maximum(1.0 - spread, 0.0)
                charges = ahead[u][3] * beside[3]
                scalar = (taper * taper) * charges * (root * root * root - 1.0)
                for c in range(3):
                    pull = scalar * apart[c]
                    held[u][c] = plus(held[u][c], pull)
                    totals[c] = plus(totals[c], pull)
            for c in range(3):
                if turn == rounds - 1:
                    plate_force[c] = plus(plate_force[c], turned(totals[c], -low))
                else:
                    pulled[low * 3 + c] = totals[c]
        for u, h in enumerate(coarse):
            for c in range(3):
                tower_force[c] = plus(tower_force[c], turned(held[u][c], LOW * h))
    return tower_force, plate_force


def sweep(listing, base, first, last, towers, plates, tower_total, plate_total, scratch):
    tower, plate, spun, pulled, tower_out, plate_out = scratch
    row = lax.broadcasted_iota(jnp.int32, (4, 128), 0)

    def step(group, _):
        places = []
        for u in range(8):
            number = first + group * 8 + u
            entry = listing[base + jnp.minimum(number, last - 1)]
            t, p = entry >> 10, entry & 1023
            tz, tc, pz, pc = t >> 6, t & 63, p >> 6, p & 63
            live = jnp.where(number < last, 1.0, 0.0)
            tower[pl.ds(u, 4, stride=8), :] = towers[
                pl.ds(tz * 256 + tc, 4, stride=64), :
            ] * jnp.where(row == 3, live, 1.0)
            plate[pl.ds(u, 4, stride=8), :] = plates[pl.ds(pz * 256 + pc, 4, stride=64), :]
            places.append((tz * 192 + tc, pz * 192 + pc))
        tower_force, plate_force = eight_pairs(tower, plate, spun, pulled)
        for c in range(3):
            tower_out[8 * c : 8 * c + 8, :] = tower_force[c]
            plate_out[8 * c : 8 * c + 8, :] = plate_force[c]
        for u, (t, p) in enumerate(places):
            tower_total[pl.ds(t, 3, stride=64), :] += tower_out[pl.ds(u, 3, stride=8), :]
            plate_total[pl.ds(p, 3, stride=64), :] -= plate_out[pl.ds(u, 3, stride=8), :]
        return 0

    groups = (jnp.maximum(last - first, 0) + 7) // 8
    lax.fori_loop(0, groups, step, 0)


def sweep_scratch():
    return [
        pltpu.VMEM((32, 128), f32),
        pltpu.VMEM((32, 128), f32),
        pltpu.VMEM((4 * LOW, 8, 128), f32),
        pltpu.VMEM((3 * LOW, 8, 128), f32),
        pltpu.VMEM((24, 128), f32),
        pltpu.VMEM((24, 128), f32),
    ]


def fill(target, block, source, lifts, strength):
    for c in range(4):
        start = block * 256 + c * 64
        values = source[c * 64 : c * 64 + 64, :]
        if c < 3:
            values = (values + lifts[c]) * SCALE if lifts[c] else values * SCALE
        elif strength:
            values = values * STRENGTH
        target[start : start + 64, :] = values


def edge_of(clusters):
    return 2.4 * (clusters / 8.0) ** (1.0 / 3.0)


def first_kernel(pairs, count, atoms, listing, own, towers, plates, totals, *scratch):
    fill(towers, 0, atoms, (0, 0, 0), True)
    fill(plates, 0, atoms, (0, 0, 0), False)
    own[...] = jnp.zeros_like(own)
    totals[...] = jnp.zeros_like(totals)
    live = count[0]

    def sort(number, counts):
        own_count, flat_count, across_count = counts
        t, p = pairs[0, number], pairs[1, number]
        block = p >> 6
        across = jnp.logical_or(block < 3, block >= 6)
        home = jnp.logical_and(block == 4, (t >> 6) == 1)
        own_place = own_count
        flat_place = SLOTS + flat_count
        across_place = 2 * SLOTS + across_count
        place = jnp.where(home, own_place, jnp.where(across, across_place, flat_place))
        plate_slot = jnp.where(across, jnp.where(block >= 6, p - 192, p), p - 192)
        entry = jnp.where(home, ((t & 63) << 10) | (p & 63), (t << 10) | plate_slot)
        listing[place] = entry
        one = jnp.int32(1)
        zero = jnp.int32(0)
        return (
            own_count + jnp.where(home, one, zero),
            flat_count + jnp.where(jnp.logical_or(home, across), zero, one),
            across_count + jnp.where(across, one, zero),
        )

    start = (jnp.int32(0), jnp.int32(0), jnp.int32(0))
    own_count, flat_count, across_count = lax.fori_loop(0, live, sort, start)
    listing[3 * SLOTS] = own_count
    listing[3 * SLOTS + 1] = flat_count
    listing[3 * SLOTS + 2] = across_count
    last = jnp.minimum(own_count, FIRST_OWN)
    sweep(listing, 0, 0, last, towers, plates, own, totals, scratch)
    own[...] += totals[...]


def second_kernel(
    listing, atoms, back, ahead, below, above, before,
    own, to_back, to_ahead, to_below, to_above,
    towers, plates, tower_total, plate_total, *scratch,
):
    edge = edge_of(atoms.shape[0] // 4)
    fill(towers, 0, below, (0, 0, -edge), True)
    fill(towers, 1, atoms, (0, 0, 0), True)
    fill(towers, 2, above, (0, 0, edge), True)
    fill(plates, 0, back, (0, -edge, 0), False)
    fill(plates, 1, atoms, (0, 0, 0), False)
    fill(plates, 2, ahead, (0, edge, 0), False)
    tower_total[...] = jnp.zeros_like(tower_total)
    plate_total[...] = jnp.zeros_like(plate_total)
    flat_count = listing[3 * SLOTS + 1]
    sweep(listing, SLOTS, 0, flat_count, towers, plates, tower_total, plate_total, scratch)
    own[...] = before[...] + tower_total[192:384, :] + plate_total[192:384, :]
    to_below[...] = tower_total[0:192, :]
    to_above[...] = tower_total[384:576, :]
    to_back[...] = plate_total[0:192, :]
    to_ahead[...] = plate_total[384:576, :]


def third_kernel(
    listing, atoms, below, above, left, right, before, was_below, was_above,
    own, to_left, to_right, to_below, to_above,
    towers, plates, tower_total, plate_total, *scratch,
):
    edge = edge_of(atoms.shape[0] // 4)
    fill(towers, 0, below, (0, 0, -edge), True)
    fill(towers, 1, atoms, (0, 0, 0), True)
    fill(towers, 2, above, (0, 0, edge), True)
    for along in range(3):
        fill(plates, along, left.at[along], (-edge, (along - 1) * edge, 0), False)
        fill(plates, 3 + along, right.at[along], (edge, (along - 1) * edge, 0), False)
    tower_total[0:192, :] = was_below[...]
    tower_total[192:384, :] = before[...]
    tower_total[384:576, :] = was_above[...]
    plate_total[...] = jnp.zeros_like(plate_total)
    across_count = listing[3 * SLOTS + 2]
    sweep(listing, 2 * SLOTS, 0, across_count, towers, plates, tower_total, plate_total, scratch)
    own[...] = tower_total[192:384, :]
    to_below[...] = tower_total[0:192, :]
    to_above[...] = tower_total[384:576, :]
    for along in range(3):
        to_left[along] = plate_total[along * 192 : along * 192 + 192, :]
        to_right[along] = plate_total[(3 + along) * 192 : (4 + along) * 192, :]


def fourth_kernel(listing, atoms, before, own, towers, plates, totals, *scratch):
    fill(towers, 0, atoms, (0, 0, 0), True)
    fill(plates, 0, atoms, (0, 0, 0), False)
    own[...] = before[...]
    totals[...] = jnp.zeros_like(totals)
    own_count = listing[3 * SLOTS]
    sweep(listing, 0, FIRST_OWN, own_count, towers, plates, own, totals, scratch)
    own[...] += totals[...]


def bond_kernel(atoms, velocities, inverse_mass, bond_partner, *refs):
    parts, (forces, moved) = refs[:-2], refs[-2:]
    rows = 8
    lane = lax.broadcasted_iota(jnp.int32, (rows, 128), 1)
    heads = lane - lane % 4
    corners = [heads + k for k in range(4)]

    def taken(values, index):
        return jnp.take_along_axis(values, index, axis=1)

    def step(tile, _):
        first = pl.multiple_of(tile * rows, rows)
        partner = bond_partner[pl.ds(first, rows), :]
        mass = inverse_mass[pl.ds(first, rows), :]
        hydro = partner != lane
        hits = [taken(partner, corner) == lane for corner in corners]
        bond, shift = [], []
        for c in range(3):
            place = pl.ds(c * 64 + first, rows)
            force = parts[0][place, :]
            for part in parts[1:]:
                force = force + part[place, :]
            forces[place, :] = force
            kicked = velocities[place, :] + TIME_STEP * FORCE_UNIT * mass * force
            shift.append(TIME_STEP * kicked)
            coords = atoms[place, :]
            bond.append(coords - taken(coords, partner))
        square = bond[0] * bond[0] + bond[1] * bond[1] + bond[2] * bond[2]
        paired = mass + taken(mass, partner)
        for sweep_number in range(ITERS):
            gap = [bond[c] + (shift[c] - taken(shift[c], partner)) for c in range(3)]
            excess = gap[0] * gap[0] + gap[1] * gap[1] + gap[2] * gap[2] - square
            along = gap[0] * bond[0] + gap[1] * bond[1] + gap[2] * bond[2]
            slope = 2.0 * along * paired
            factor = jnp.where(hydro, excess / jnp.where(hydro, slope, 1.0), 0.0)
            for c in range(3):
                delta = factor * bond[c]
                back = None
                for corner, hit in zip(corners, hits):
                    back = plus(back, jnp.where(hit, taken(delta, corner), 0.0))
                shift[c] = shift[c] + mass * (back - delta)
        for c in range(3):
            moved[pl.ds(c * 64 + first, rows), :] = shift[c] / TIME_STEP
        return 0

    lax.fori_loop(0, inverse_mass.shape[0] // rows, step, 0)


def planes(count=None):
    shape = (192, 128) if count is None else (count, 192, 128)
    return jax.ShapeDtypeStruct(shape, f32)


def run(kernel, outs, scalars, arrays, scratch, microseconds):
    smem = pl.BlockSpec(memory_space=pltpu.SMEM)
    vmem = pl.BlockSpec(memory_space=pltpu.VMEM)
    return pl.pallas_call(
        kernel,
        out_shape=outs,
        in_specs=[smem] * len(scalars) + [vmem] * len(arrays),
        out_specs=[smem if out.dtype == jnp.int32 else vmem for out in outs],
        scratch_shapes=scratch,
        compiler_params=pltpu.CompilerParams(vmem_limit_bytes=32 * 1024 * 1024),
        cost_estimate=pl.CostEstimate(
            flops=int(microseconds * 4e6), bytes_accessed=int(microseconds * 3e6), transcendentals=0
        ),
    )(*scalars, *arrays)


def local(atoms, velocities, inverse_mass, bond_partner, cluster_pairs, pair_count):
    own = atoms.reshape(256, 128)
    blocks = lambda count, rows: pltpu.VMEM((count * rows, 128), f32)
    back = passed_along(own, "gy", 1)
    ahead = passed_along(own, "gy", -1)
    below = passed_along(own, "gz", 1)
    above = passed_along(own, "gz", -1)
    triple = jnp.stack([back, own, ahead])
    left = passed_along(triple, "gx", 1)
    right = passed_along(triple, "gx", -1)
    listing, part = run(
        first_kernel,
        [jax.ShapeDtypeStruct((3 * SLOTS + 8,), jnp.int32), planes()],
        [cluster_pairs.reshape(2, -1), pair_count.reshape(1)],
        [own],
        [blocks(1, 256), blocks(1, 256), blocks(1, 192)] + sweep_scratch(),
        4,
    )
    part, to_back, to_ahead, to_below, to_above = run(
        second_kernel,
        [planes()] * 5,
        [listing],
        [own, back, ahead, below, above, part],
        [blocks(3, 256), blocks(3, 256), blocks(3, 192), blocks(3, 192)] + sweep_scratch(),
        6,
    )
    part, to_left, to_right, to_below, to_above = run(
        third_kernel,
        [planes(), planes(3), planes(3), planes(), planes()],
        [listing],
        [own, below, above, left, right, part, to_below, to_above],
        [blocks(3, 256), blocks(6, 256), blocks(3, 192), blocks(6, 192)] + sweep_scratch(),
        4,
    )
    from_right = passed_along(to_left, "gx", -1)
    from_left = passed_along(to_right, "gx", 1)
    from_above = passed_along(to_below, "gz", -1)
    from_below = passed_along(to_above, "gz", 1)
    (part,) = run(
        fourth_kernel,
        [planes()],
        [listing],
        [own, part],
        [blocks(1, 256), blocks(1, 256), blocks(1, 192)] + sweep_scratch(),
        6,
    )
    from_ahead = passed_along(to_back + from_left[0] + from_right[0], "gy", -1)
    from_back = passed_along(to_ahead + from_left[2] + from_right[2], "gy", 1)
    forces, moved = run(
        bond_kernel,
        [planes(), planes()],
        [],
        [
            own,
            velocities.reshape(192, 128),
            inverse_mass.reshape(64, 128),
            bond_partner.reshape(64, 128),
            part,
            from_left[1],
            from_right[1],
            from_above,
            from_below,
            from_ahead,
            from_back,
        ],
        [],
        2,
    )
    return (forces.reshape(3, 1, 1, 64, 128), moved.reshape(3, 1, 1, 64, 128))


def solution(mesh):
    return jax.shard_map(
        local,
        mesh=mesh,
        in_specs=(
            P(None, "gx", "gy", "gz", None),
            P(None, "gx", "gy", "gz", None),
            P("gx", "gy", "gz", None),
            P("gx", "gy", "gz", None),
            P(None, "gx", "gy", "gz"),
            P("gx", "gy", "gz"),
        ),
        out_specs=(P(None, "gx", "gy", "gz", None), P(None, "gx", "gy", "gz", None)),
        check_vma=False,
    )
```

time: 160 us -> 69.3 us (0.43)
  the two profiles are of different devices: /device:TPU:133 before, /device:TPU:28 now
where the time goes in v1:
time: 69.3 us; the launch traced here: 70.7 us
  Pallas kernels  36.1 us (52%)
  starting transfers between devices  19.6 us (28%)
  waiting for transfers between devices  12.5 us (18%)
  between operations  1.46 us (2%)
  other arithmetic  1.03 us (1%)
    pallas_call x5, Pallas kernels, run(): pl.pallas_call(kernel, out_shape=outs, in_specs=[smem] * len(scalars) + [...  36.1 us
    ppermute x12, starting transfers between devices, passed_along(): return lax.ppermute(value, axis, pairs)  19.6 us
    ppermute x12, waiting for transfers between devices, passed_along(): return lax.ppermute(value, axis, pairs)  12.5 us
  transfers between devices with their start and end apart: 12, of which 3 were waited for; matrix products, arithmetic and copies ran while one was open for 0% of the time, Pallas kernels for 37%

profile of v1, /device:TPU:28, one launch (start us, length us, event | category | flops | bytes accessed | tf_op | source)
XLA Modules:
  0.0 70.7 jit_solution(14433256219885602874)
XLA Ops:
  0.6 0.6 collective-permute-start.3
  1.2 5.1 %collective-permute-start.2 = (f32[256,128]{1,0:T(8,128)}, f32[256,128]{1,0:T(8,128)S(1)}, u32[]{:S(2)}, u32[]{:S(2)}) collective-permute-start(f32[256,128]{1,0:T(8,128)} %bitcast.43), channel_id=1, source_target_pairs={{0,8},{8,16},{16,24},{24,32},{32,40},{40,48},{48,56},{56,0},{1,9},... | collective-permute-start | bytes 393224 | tf_op jit(solution)/shard_map/ppermute | solution.py:28
  6.3 4.6 %collective-permute-done.3.ahead = f32[256,128]{1,0:T(8,128)S(1)} collective-permute-done((f32[256,128]{1,0:T(8,128)}, f32[256,128]{1,0:T(8,128)S(1)}, u32[]{:S(2)}, u32[]{:S(2)}) %collective-permute-start.3) | collective-permute-done | bytes 131104 | tf_op jit(solution)/shard_map/ppermute | solution.py:28
  10.9 0.0 collective-permute-done.2.back
  10.9 1.0 %pad_maximum_fusion = f32[3,256,128]{2,1,0:T(8,128)S(1)} fusion(f32[1,256,128]{2,1,0:T(8,128)S(1)} %bitcast.52, f32[1,256,128]{2,1,0:T(8,128)} %bitcast.44, f32[1,256,128]{2,1,0:T(8,128)S(1)} %bitcast.53), kind=kLoop, calls=%fused_computation | loop fusion | flops 196608 | bytes 786432 | tf_op jit(solution)/shard_map/stack | solution.py:308
  11.9 0.1 collective-permute-start.5
  12.0 0.5 collective-permute-start.4
  12.5 5.9 %collective-permute-start.1 = (f32[256,128]{1,0:T(8,128)S(1)}, f32[256,128]{1,0:T(8,128)S(1)}, u32[]{:S(2)}, u32[]{:S(2)}) collective-permute-start(f32[256,128]{1,0:T(8,128)S(1)} %bitcast.45), channel_id=1, source_target_pairs={{0,7},{1,0},{2,1},{3,2},{4,3},{5,4},{6,5},{7,6},{8,15},{9,8},{10,9... | collective-permute-start | bytes 393224 | tf_op jit(solution)/shard_map/ppermute | solution.py:28
  18.4 0.0 collective-permute-start
  19.0 9.8 %shard_map.77 = (s32[824]{0:T(1024)S(1)}, f32[192,128]{1,0:T(8,128)S(1)}) custom-call(s32[2,256]{1,0:T(2,128)S(1)} %bitcast.57, s32[1]{0:T(128)} %bitcast.41.count, f32[256,128]{1,0:T(8,128)S(1)} %bitcast.47), custom_call_target="tpu_custom_call" | custom-call | flops 16000000 | bytes 12000000 | tf_op jit(solution)/shard_map/pallas_call | solution.py:288
  28.9 0.0 collective-permute-done.1.above
  28.9 0.0 collective-permute-done.below
  28.9 7.5 %shard_map.78 = (f32[192,128]{1,0:T(8,128)S(1)}, f32[192,128]{1,0:T(8,128)S(1)}, f32[192,128]{1,0:T(8,128)S(1)}, f32[192,128]{1,0:T(8,128)S(1)}, f32[192,128]{1,0:T(8,128)S(1)}) custom-call(s32[824]{0:T(1024)S(1)} %get-tuple-element.16.listing, f32[256,128]{1,0:T(8,128)S(1)} %bitcast.48, f32[256,128]{1,0:T(8,128)S(1)} %collective-permute-done.2.back, ...), custom_call_target="tpu_custom_call" | custom-call | flops 24000000 | bytes 18000000 | tf_op jit(solution)/shard_map/pallas_call | solution.py:288
  36.4 0.0 collective-permute-done.5.right
  36.4 0.0 collective-permute-done.4.left
  36.5 6.1 %shard_map.79 = (f32[192,128]{1,0:T(8,128)S(1)}, f32[3,192,128]{2,1,0:T(8,128)S(1)}, f32[3,192,128]{2,1,0:T(8,128)S(1)}, f32[192,128]{1,0:T(8,128)S(1)}, f32[192,128]{1,0:T(8,128)S(1)}) custom-call(s32[824]{0:T(1024)S(1)} %get-tuple-element.16.listing, f32[256,128]{1,0:T(8,128)S(1)} %bitcast.49, f32[256,128]{1,0:T(8,128)S(1)} %collective-permute-done.below, ...), custom_call_target="tpu_custom_call" | custom-call | flops 16000000 | bytes 12000000 | tf_op jit(solution)/shard_map/pallas_call | solution.py:288
  42.6 0.1 collective-permute-start.6
  42.7 1.7 %collective-permute-start.7 = (f32[3,192,128]{2,1,0:T(8,128)S(1)}, f32[3,192,128]{2,1,0:T(8,128)S(1)}, u32[]{:S(2)}, u32[]{:S(2)}) collective-permute-start(f32[3,192,128]{2,1,0:T(8,128)S(1)} %get-tuple-element.23), channel_id=1, source_target_pairs={{0,192},{64,0},{128,64},{192,128},{1,193},{65,1},{129,65},{193,129... | collective-permute-start | bytes 884744 | tf_op jit(solution)/shard_map/ppermute | solution.py:28
  44.4 0.0 collective-permute-start.8
  44.4 2.0 %collective-permute-start.9 = (f32[192,128]{1,0:T(8,128)S(1)}, f32[192,128]{1,0:T(8,128)S(1)}, u32[]{:S(2)}, u32[]{:S(2)}) collective-permute-start(f32[192,128]{1,0:T(8,128)S(1)} %get-tuple-element.25), channel_id=1, source_target_pairs={{0,1},{1,2},{2,3},{3,4},{4,5},{5,6},{6,7},{7,0},{8,9},{9,10},{10,1... | collective-permute-start | bytes 294920 | tf_op jit(solution)/shard_map/ppermute | solution.py:28
  46.4 8.9 %shard_map.80.refs_0_ = f32[192,128]{1,0:T(8,128)S(1)} custom-call(s32[824]{0:T(1024)S(1)} %get-tuple-element.16.listing, f32[256,128]{1,0:T(8,128)S(1)} %bitcast.50, f32[192,128]{1,0:T(8,128)S(1)} %get-tuple-element.21.before), custom_call_target="tpu_custom_call" | custom-call | flops 24000000 | bytes 18000000 | tf_op jit(solution)/shard_map/pallas_call | solution.py:288
  55.3 0.0 collective-permute-done.6
  55.3 0.0 collective-permute-done.7
  55.4 3.4 %collective-permute-start.11 = (f32[192,128]{1,0:T(8,128)S(1)}, f32[192,128]{1,0:T(8,128)S(1)}, u32[]{:S(2)}, u32[]{:S(2)}) collective-permute-start(f32[192,128]{1,0:T(8,128)S(1)} %get-tuple-element.32), channel_id=1, source_target_pairs={{0,8},{8,16},{16,24},{24,32},{32,40},{40,48},{48,56},{56,0},{1,9},... | collective-permute-start | bytes 294920 | tf_op jit(solution)/shard_map/ppermute | solution.py:28
  58.7 0.3 collective-permute-start.10
  59.0 0.0 copy-start.2
  59.0 0.0 copy-start.3
  59.0 0.0 collective-permute-done.8.refs_3_
  59.1 0.0 collective-permute-done.9.refs_4_
  59.1 2.5 %collective-permute-done.11.refs_6_ = f32[192,128]{1,0:T(8,128)S(1)} collective-permute-done((f32[192,128]{1,0:T(8,128)S(1)}, f32[192,128]{1,0:T(8,128)S(1)}, u32[]{:S(2)}, u32[]{:S(2)}) %collective-permute-start.11) | collective-permute-done | bytes 98336 | tf_op jit(solution)/shard_map/ppermute | solution.py:28
  61.6 5.4 %collective-permute-done.10.refs_5_ = f32[192,128]{1,0:T(8,128)S(1)} collective-permute-done((f32[192,128]{1,0:T(8,128)S(1)}, f32[192,128]{1,0:T(8,128)S(1)}, u32[]{:S(2)}, u32[]{:S(2)}) %collective-permute-start.10) | collective-permute-done | bytes 98336 | tf_op jit(solution)/shard_map/ppermute | solution.py:28
  67.0 3.7 %shard_map.81 = (f32[192,128]{1,0:T(8,128)}, f32[192,128]{1,0:T(8,128)}) custom-call(f32[256,128]{1,0:T(8,128)S(1)} %bitcast.51, f32[192,128]{1,0:T(8,128)S(1)} %bitcast.54, f32[64,128]{1,0:T(8,128)S(1)} %bitcast.55, s32[64,128]{1,0:T(8,128)S(1)} %bitcast.56, f32[192,128]{1,0:T(8,128)S(1)} %shard_map.80.refs_0_, f32[192,128]{1,0:T(8,128)S(1)} %slice_bitcast_fusion.5.refs_1_, ...), custom_call_target="tpu_custom_call" | custom-call | flops 8000000 | bytes 6000000 | tf_op jit(solution)/shard_map/pallas_call | solution.py:288
  (12 shorter events, 0.1 us)
Async XLA Ops:
  0.6 10.3 %collective-permute-start.3 = (f32[256,128]{1,0:T(8,128)}, f32[256,128]{1,0:T(8,128)S(1)}, u32[]{:S(2)}, u32[]{:S(2)}) collective-permute-start(f32[256,128]{1,0:T(8,128)} %bitcast.42), channel_id=1, source_target_pairs={{0,56},{8,0},{16,8},{24,16},{32,24},{40,32},{48,40},{56,48},{1,57}... | collective-permute-start | bytes 393224 | tf_op jit(solution)/shard_map/ppermute | solution.py:28
  1.2 9.7 %collective-permute-start.2 = (f32[256,128]{1,0:T(8,128)}, f32[256,128]{1,0:T(8,128)S(1)}, u32[]{:S(2)}, u32[]{:S(2)}) collective-permute-start(f32[256,128]{1,0:T(8,128)} %bitcast.43), channel_id=1, source_target_pairs={{0,8},{8,16},{16,24},{24,32},{32,40},{40,48},{48,56},{56,0},{1,9},... | collective-permute-start | bytes 393224 | tf_op jit(solution)/shard_map/ppermute | solution.py:28
  10.9 1.6 %copy-start = (f32[4,1,1,64,128]{4,3,2,1,0:T(8,128)S(1)}, f32[4,1,1,64,128]{4,3,2,1,0:T(8,128)}, u32[]{:S(2)}) copy-start(f32[4,1,1,64,128]{4,3,2,1,0:T(8,128)} %param.6) | copy-start | bytes 393220
  10.9 8.1 %copy-start.4 = (s32[2,1,1,256]{3,2,1,0:T(1,128)S(1)}, s32[2,1,1,256]{3,2,1,0:T(1,128)}, u32[]{:S(2)}) copy-start(s32[2,1,1,256]{3,2,1,0:T(1,128)} %param.10) | copy-start | bytes 6148
  11.9 24.5 %collective-permute-start.5 = (f32[3,256,128]{2,1,0:T(8,128)S(1)}, f32[3,256,128]{2,1,0:T(8,128)S(1)}, u32[]{:S(2)}, u32[]{:S(2)}) collective-permute-start(f32[3,256,128]{2,1,0:T(8,128)S(1)} %pad_maximum_fusion), channel_id=1, source_target_pairs={{0,192},{64,0},{128,64},{192,128},{1,193},{65,1},{129,65},{193,129... | collective-permute-start | bytes 1179656 | tf_op jit(solution)/shard_map/ppermute | solution.py:28
  12.0 24.4 %collective-permute-start.4 = (f32[3,256,128]{2,1,0:T(8,128)S(1)}, f32[3,256,128]{2,1,0:T(8,128)S(1)}, u32[]{:S(2)}, u32[]{:S(2)}) collective-permute-start(f32[3,256,128]{2,1,0:T(8,128)S(1)} %pad_maximum_fusion), channel_id=1, source_target_pairs={{0,64},{64,128},{128,192},{192,0},{1,65},{65,129},{129,193},{193,1... | collective-permute-start | bytes 1179656 | tf_op jit(solution)/shard_map/ppermute | solution.py:28
  12.5 16.4 %collective-permute-start.1 = (f32[256,128]{1,0:T(8,128)S(1)}, f32[256,128]{1,0:T(8,128)S(1)}, u32[]{:S(2)}, u32[]{:S(2)}) collective-permute-start(f32[256,128]{1,0:T(8,128)S(1)} %bitcast.45), channel_id=1, source_target_pairs={{0,7},{1,0},{2,1},{3,2},{4,3},{5,4},{6,5},{7,6},{8,15},{9,8},{10,9... | collective-permute-start | bytes 393224 | tf_op jit(solution)/shard_map/ppermute | solution.py:28
  18.4 10.5 %collective-permute-start = (f32[256,128]{1,0:T(8,128)S(1)}, f32[256,128]{1,0:T(8,128)S(1)}, u32[]{:S(2)}, u32[]{:S(2)}) collective-permute-start(f32[256,128]{1,0:T(8,128)S(1)} %bitcast.46), channel_id=1, source_target_pairs={{0,1},{1,2},{2,3},{3,4},{4,5},{5,6},{6,7},{7,0},{8,9},{9,10},{10,1... | collective-permute-start | bytes 393224 | tf_op jit(solution)/shard_map/ppermute | solution.py:28
  42.6 12.8 %collective-permute-start.6 = (f32[3,192,128]{2,1,0:T(8,128)S(1)}, f32[3,192,128]{2,1,0:T(8,128)S(1)}, u32[]{:S(2)}, u32[]{:S(2)}) collective-permute-start(f32[3,192,128]{2,1,0:T(8,128)S(1)} %get-tuple-element.22), channel_id=1, source_target_pairs={{0,64},{64,128},{128,192},{192,0},{1,65},{65,129},{129,193},{193,1... | collective-permute-start | bytes 884744 | tf_op jit(solution)/shard_map/ppermute | solution.py:28
  42.7 12.7 %collective-permute-start.7 = (f32[3,192,128]{2,1,0:T(8,128)S(1)}, f32[3,192,128]{2,1,0:T(8,128)S(1)}, u32[]{:S(2)}, u32[]{:S(2)}) collective-permute-start(f32[3,192,128]{2,1,0:T(8,128)S(1)} %get-tuple-element.23), channel_id=1, source_target_pairs={{0,192},{64,0},{128,64},{192,128},{1,193},{65,1},{129,65},{193,129... | collective-permute-start | bytes 884744 | tf_op jit(solution)/shard_map/ppermute | solution.py:28
  44.4 14.7 %collective-permute-start.8 = (f32[192,128]{1,0:T(8,128)S(1)}, f32[192,128]{1,0:T(8,128)S(1)}, u32[]{:S(2)}, u32[]{:S(2)}) collective-permute-start(f32[192,128]{1,0:T(8,128)S(1)} %get-tuple-element.24), channel_id=1, source_target_pairs={{0,7},{1,0},{2,1},{3,2},{4,3},{5,4},{6,5},{7,6},{8,15},{9,8},{10,9... | collective-permute-start | bytes 294920 | tf_op jit(solution)/shard_map/ppermute | solution.py:28
  44.4 14.7 %collective-permute-start.9 = (f32[192,128]{1,0:T(8,128)S(1)}, f32[192,128]{1,0:T(8,128)S(1)}, u32[]{:S(2)}, u32[]{:S(2)}) collective-permute-start(f32[192,128]{1,0:T(8,128)S(1)} %get-tuple-element.25), channel_id=1, source_target_pairs={{0,1},{1,2},{2,3},{3,4},{4,5},{5,6},{6,7},{7,0},{8,9},{9,10},{10,1... | collective-permute-start | bytes 294920 | tf_op jit(solution)/shard_map/ppermute | solution.py:28
  55.4 6.2 %collective-permute-start.11 = (f32[192,128]{1,0:T(8,128)S(1)}, f32[192,128]{1,0:T(8,128)S(1)}, u32[]{:S(2)}, u32[]{:S(2)}) collective-permute-start(f32[192,128]{1,0:T(8,128)S(1)} %get-tuple-element.32), channel_id=1, source_target_pairs={{0,8},{8,16},{16,24},{24,32},{32,40},{40,48},{48,56},{56,0},{1,9},... | collective-permute-start | bytes 294920 | tf_op jit(solution)/shard_map/ppermute | solution.py:28
  58.7 8.2 %collective-permute-start.10 = (f32[192,128]{1,0:T(8,128)S(1)}, f32[192,128]{1,0:T(8,128)S(1)}, u32[]{:S(2)}, u32[]{:S(2)}) collective-permute-start(f32[192,128]{1,0:T(8,128)S(1)} %get-tuple-element.33), channel_id=1, source_target_pairs={{0,56},{8,0},{16,8},{24,16},{32,24},{40,32},{48,40},{56,48},{1,57}... | collective-permute-start | bytes 294920 | tf_op jit(solution)/shard_map/ppermute | solution.py:28
  59.0 8.0 %copy-start.1 = (f32[3,1,1,64,128]{4,3,2,1,0:T(8,128)S(1)}, f32[3,1,1,64,128]{4,3,2,1,0:T(8,128)}, u32[]{:S(2)}) copy-start(f32[3,1,1,64,128]{4,3,2,1,0:T(8,128)} %param.7) | copy-start | bytes 294916
  59.0 8.0 %copy-start.2 = (f32[1,1,64,128]{3,2,1,0:T(8,128)S(1)}, f32[1,1,64,128]{3,2,1,0:T(8,128)}, u32[]{:S(2)}) copy-start(f32[1,1,64,128]{3,2,1,0:T(8,128)} %param.8) | copy-start | bytes 98308
  59.0 8.0 %copy-start.3 = (s32[1,1,64,128]{3,2,1,0:T(8,128)S(1)}, s32[1,1,64,128]{3,2,1,0:T(8,128)}, u32[]{:S(2)}) copy-start(s32[1,1,64,128]{3,2,1,0:T(8,128)} %param.9) | copy-start | bytes 98308
